TPU v7x, 256 devices: a whole 4x4x8 slice. The times are simulated.
256 devices in a mesh: vol: 16 (over x, y), sp: 16 (over z, core).
Axes of the slice: x: 4, y: 4, z: 8, core: 2. Of those that a mesh axis runs over, the one named last changes fastest.
Arguments:
- volume: bfloat16 [16, 16, 32, 32, 128], P('vol', 'sp'), may hold values from -6 to 6
- conv_weight: bfloat16 [3, 3, 3, 128, 256], replicated, may hold values from -0.109375 to 0.109375
- group_weight: bfloat16 [3, 3, 8, 256], replicated, may hold values from -0.75 to 0.75
- slice_count: int32 [16], P('vol'), may hold values from 5 to 16
- pooled_grad: float32 [16, 256], P('vol'), may hold values from -48 to 48
Outputs:
- grad_conv: float32 [3, 3, 3, 128, 256], P(None, None, None, None, 'sp')
- grad_group: float32 [3, 3, 8, 256], P(None, None, None, 'sp')
All inputs are finite; a program needn't handle non-finite values.
Results may differ from a plain program's by a relative error of at most 0.028.
The roundings to bfloat16 on the way count: a program that leaves them out, or rounds other values in their place, can miss the bound.
Values may be sent and summed in bfloat16 or wider, within the bound.
A program may use at most 128 MiB of HBM per device.

v0:
```python
import jax
import jax.numpy as jnp
from jax import lax
from jax.experimental import pallas as pl
from jax.experimental.pallas import tpu as pltpu
from jax.sharding import PartitionSpec as P

BF16 = jnp.bfloat16
F32 = jnp.float32
REDUCERS = 15


def remote(src, dst, send, recv, device):
    return pltpu.make_async_remote_copy(
        src_ref=src,
        dst_ref=dst,
        send_sem=send,
        recv_sem=recv,
        device_id=device,
        device_id_type=pl.DeviceIdType.MESH,
    )


def dot(left, right):
    return jnp.dot(left, right, preferred_element_type=F32)


def dot_nt(left, right):
    return lax.dot_general(left, right, (((1,), (1,)), ((), ())), preferred_element_type=F32)


def one_where(condition):
    return jnp.where(condition, 1.0, 0.0).astype(BF16)


def iota(shape, dim):
    return lax.broadcasted_iota(jnp.int32, shape, dim)


def kernel(
    vol,
    w,
    gw,
    cnt,
    pg,
    conv_out,
    group_out,
    volb,
    wv,
    xs,
    pick,
    shift,
    wg,
    hk,
    dk,
    dts,
    ggs,
    dx,
    gx,
    part,
    r1,
    s2,
    r2,
    f3,
    outb,
    loc_sem,
    halo_send,
    halo_recv,
    dx_send,
    dx_recv,
    s1_send,
    s1_recv,
    s2_send,
    s2_recv,
    s3_send,
    s3_recv,
):
    v = lax.axis_index("vol")
    sp = lax.axis_index("sp")
    x, y = lax.div(v, 4), lax.rem(v, 4)
    z, core = lax.div(sp, 2), lax.rem(sp, 2)
    sib = (v, z * 2 + 1 - core)
    far = (v, lax.rem(sp + 15 + 2 * core, 16))

    def vol_peer(i):
        return lax.rem(x + lax.div(i, 4), 4) * 4 + lax.rem(y + lax.rem(i, 4), 4)

    def z_peer(i):
        return lax.rem(z + i, 8)

    own_copy = pltpu.make_async_copy(vol, volb.at[1 + core], loc_sem.at[0])
    own_copy.start()
    w_copy = pltpu.make_async_copy(w, wv, loc_sem.at[1])
    w_copy.start()

    barrier = pltpu.get_barrier_semaphore()

    def greet(device):
        pl.semaphore_signal(barrier, inc=1, device_id=device, device_id_type=pl.DeviceIdType.MESH)

    greet(sib)
    greet(far)

    def greet_vol(i, carry):
        greet((vol_peer(i), sp))
        return carry

    def greet_z(i, carry):
        greet((v, z_peer(i) * 2 + core))
        return carry

    lax.fori_loop(1, 16, greet_vol, 0)
    lax.fori_loop(1, 8, greet_z, 0)

    m = iota((384, 256), 0)
    tap, within = lax.div(m, 128), lax.rem(m, 128)
    row = 2 * lax.div(lax.rem(within, 64), 16) + lax.div(within, 64)
    col = 2 * lax.rem(within, 16) + tap - 1
    pick[...] = one_where((iota((384, 256), 1) == row * 32 + col) & (col >= 0))

    pl.semaphore_wait(barrier, 24)
    to_sib = remote(vol, volb.at[1 + core], halo_send.at[0], halo_recv.at[0], sib)
    to_far = remote(vol, volb.at[3 - 3 * core], halo_send.at[1], halo_recv.at[1], far)
    to_far.start()
    to_sib.start()

    m, n = iota((256, 256), 0), iota((256, 256), 1)
    in_row = lax.rem(m, 16)
    shift[0] = one_where((n == m - 1) & (in_row != 0))
    shift[1] = one_where((n == m + 1) & (in_row != 15))
    same_group = lax.div(m, 8) == lax.div(n, 8)
    for jk in range(9):
        tiled = jnp.broadcast_to(gw[jk].astype(F32)[None], (32, 8, 256)).reshape(256, 256)
        wg[jk] = jnp.where(same_group, tiled, 0.0).astype(BF16)
    for k in range(3):
        hk[k, 0:16, :] = jnp.zeros((16, 256), BF16)
        hk[k, 272:288, :] = jnp.zeros((16, 256), BF16)
        dk[k, 0:16, :] = jnp.zeros((16, 256), BF16)
        dk[k, 272:288, :] = jnp.zeros((16, 256), BF16)

    def windows(slot, inside):
        xs[slot, 0:16, 0:384] = jnp.zeros((16, 384), BF16)
        xs[slot, :, 1152:1280] = jnp.zeros((272, 128), BF16)
        for block in range(4):
            picked = dot(pick[...], volb[slot, 256 * block : 256 * block + 256, :])
            if inside is not None:
                picked = picked * inside
            picked = picked.astype(BF16)
            for e in range(3):
                even = picked[e * 128 : e * 128 + 64]
                odd = picked[e * 128 + 64 : e * 128 + 128]
                for b, rows, offset in ((0, odd, 16), (1, even, 0), (2, odd, 0)):
                    lane = (b * 3 + e) * 128
                    start = 64 * block + offset
                    xs[slot, start : start + 64, lane : lane + 128] = rows

    at_low = jnp.where(z == 0, 0.0, 1.0)
    at_high = jnp.where(z == 7, 0.0, 1.0)
    far_inside = jnp.where(core == 0, at_low, at_high)
    beyond_inside = jnp.where(core == 0, at_high, at_low)

    own_copy.wait()
    windows(1 + core, None)
    remote(vol, volb.at[2 - core], halo_send.at[0], halo_recv.at[0], sib).wait_recv()
    windows(2 - core, None)
    remote(vol, volb.at[3 * core], halo_send.at[1], halo_recv.at[1], far).wait_recv()
    relay = remote(
        volb.at[3 * core], volb.at[3 * core], halo_send.at[2], halo_recv.at[2], sib
    )
    relay.start()
    windows(3 * core, far_inside)
    w_copy.wait()

    pre = dot(xs[core, 0:256, 0:1152], wv[0])
    pre = pre + dot(xs[core + 1, 0:256, 0:1152], wv[1])
    pre = pre + dot(xs[core + 2, 0:256, 0:1152], wv[2])

    count = cnt[0]
    live = jnp.where(sp < count, 1.0, 0.0)
    hidden = (jnp.maximum(pre, 0.0) * live).astype(BF16)
    hk[1, 16:272, :] = hidden
    hk[0, 16:272, :] = dot(shift[0], hidden).astype(BF16)
    hk[2, 16:272, :] = dot(shift[1], hidden).astype(BF16)
    summed = hidden.astype(F32)
    for j in range(3):
        for k in range(3):
            summed = summed + dot(hk[k, 16 * j : 16 * j + 256, :], wg[3 * j + k])
    scale = 1.0 / jnp.full((1, 256), count.astype(F32) * 256.0)
    cotangent = pg[...] * live * scale
    d_wide = jnp.where(summed > 0, cotangent, 0.0)
    d_summed = d_wide.astype(BF16)
    dk[1, 16:272, :] = d_summed
    dk[0, 16:272, :] = dot(shift[0], d_summed).astype(BF16)
    dk[2, 16:272, :] = dot(shift[1], d_summed).astype(BF16)
    d_hidden = d_summed.astype(F32)
    for j in range(3):
        for k in range(3):
            lines = dk[2 - k, 16 * (2 - j) : 16 * (2 - j) + 256, :]
            d_hidden = d_hidden + dot_nt(lines, wg[3 * j + k])
    d_pre = jnp.where(pre > 0, d_hidden, 0.0) * live
    turned = d_pre.T.astype(BF16)
    for t in range(8):
        for c in range(2):
            start = 16 * (2 * t + c)
            dts[c, 16 * t : 16 * t + 16, :] = turned[start : start + 16, :]
    swap_d = remote(dts.at[1 - core], dx, dx_send.at[0], dx_recv.at[0], sib)
    swap_d.start()

    d_turned = d_wide.T.astype(BF16)
    fold = one_where(lax.rem(iota((256, 128), 0), 8) == lax.rem(iota((256, 128), 1), 8))
    lane_tap = lax.div(iota((256, 128), 1), 8)
    grouped = jnp.zeros((256, 128), F32)
    for j in range(3):
        for k in range(3):
            full = dot(d_turned, hk[k, 16 * j : 16 * j + 256, :])
            kept = jnp.where(same_group, full, 0.0).astype(BF16)
            grouped = jnp.where(lane_tap == 3 * j + k, dot(kept, fold), grouped)
    grouped = grouped.astype(BF16)
    for t in range(8):
        for c in range(2):
            start = 16 * (2 * t + c)
            ggs[c, 16 * t : 16 * t + 16, :] = grouped[start : start + 16, :]
    swap_g = remote(ggs.at[1 - core], gx, dx_send.at[1], dx_recv.at[1], sib)
    swap_g.start()

    remote(
        volb.at[3 - 3 * core], volb.at[3 - 3 * core], halo_send.at[2], halo_recv.at[2], sib
    ).wait_recv()
    windows(3 - 3 * core, beyond_inside)
    swap_d.wait_recv()
    swap_g.wait_recv()

    def partial(i, carry):
        to = vol_peer(i)

        @pl.when(to < REDUCERS)
        def _():
            a = lax.div(to, 5)
            lanes = pl.ds(pl.multiple_of(lax.rem(to, 5) * 256, 256), 256)
            total = dot(dts[core], xs[core + a, 0:256, lanes])
            total = total + dot(dx[...], xs[1 - core + a, 0:256, lanes])
            low = total[:, 0:128].astype(BF16)
            extra = (ggs[core].astype(F32) + gx[...].astype(F32)) * jnp.where(
                to == REDUCERS - 1, 1.0, 0.0
            )
            high = (total[:, 128:256] + extra).astype(BF16)

            @pl.when(i == 0)
            def _():
                r1[v, 0] = low
                r1[v, 1] = high

            @pl.when(i > 0)
            def _():
                part[to, 0] = low
                part[to, 1] = high
                remote(
                    part.at[to], r1.at[v], s1_send.at[to], s1_recv.at[v], (to, sp)
                ).start()

        return carry

    lax.fori_loop(0, 16, partial, 0)

    @pl.when(v < REDUCERS)
    def _():
        def add(i, carry):
            source = vol_peer(i)
            remote(
                part.at[0], r1.at[source], s1_send.at[0], s1_recv.at[source], (source, sp)
            ).wait_recv()
            return tuple(carry[h] + r1[source, h].astype(F32) for h in range(2))

        start = tuple(r1[v, h].astype(F32) for h in range(2))
        sums = lax.fori_loop(1, 16, add, start)
        for t in range(8):
            for h in range(2):
                s2[t, h] = sums[h][16 * t : 16 * t + 16, :]

        def send_z(i, carry):
            to = z_peer(i)
            remote(
                s2.at[to], r2.at[z], s2_send.at[to], s2_recv.at[z], (v, to * 2 + core)
            ).start()
            return carry

        lax.fori_loop(1, 8, send_z, 0)

        def add_z(i, carry):
            source = z_peer(i)
            remote(
                s2.at[0], r2.at[source], s2_send.at[0], s2_recv.at[source], (v, source * 2 + core)
            ).wait_recv()
            return carry + r2[source]

        final = lax.fori_loop(1, 8, add_z, s2[z])
        f3[...] = final
        outb[v] = final

        def spread(i, carry):
            to = vol_peer(i)
            remote(f3, outb.at[v], s3_send.at[to], s3_recv.at[v], (to, sp)).start()
            return carry

        lax.fori_loop(1, 16, spread, 0)

    def collect(i, carry):
        source = vol_peer(i)

        @pl.when(source < REDUCERS)
        def _():
            remote(
                f3, outb.at[source], s3_send.at[0], s3_recv.at[source], (source, sp)
            ).wait_recv()

        return carry

    lax.fori_loop(1, 16, collect, 0)
    for a in range(3):
        for t in range(9):
            conv_out[9 * a + t] = outb[5 * a + t // 2, t % 2]
    last = jnp.concatenate([outb[REDUCERS - 1, 1], jnp.zeros((112, 128), F32)], axis=0)
    group_out[...] = last.T[0:72, 0:16]

    to_sib.wait_send()
    to_far.wait_send()
    relay.wait_send()
    swap_d.wait_send()
    swap_g.wait_send()

    def drain_vol(i, carry):
        to = vol_peer(i)

        @pl.when(to < REDUCERS)
        def _():
            remote(part.at[to], r1.at[v], s1_send.at[to], s1_recv.at[v], (to, sp)).wait_send()

        @pl.when(v < REDUCERS)
        def _():
            remote(f3, outb.at[v], s3_send.at[to], s3_recv.at[v], (to, sp)).wait_send()

        return carry

    lax.fori_loop(1, 16, drain_vol, 0)

    @pl.when(v < REDUCERS)
    def _():
        def drain_z(i, carry):
            to = z_peer(i)
            remote(
                s2.at[to], r2.at[z], s2_send.at[to], s2_recv.at[z], (v, to * 2 + core)
            ).wait_send()
            return carry

        lax.fori_loop(1, 8, drain_z, 0)


def local(volume, conv_weight, group_weight, slice_count, pooled_grad):
    vmem = pl.BlockSpec(memory_space=pltpu.VMEM)
    smem = pl.BlockSpec(memory_space=pltpu.SMEM)
    hbm = pl.BlockSpec(memory_space=pl.ANY)
    dma = pltpu.SemaphoreType.DMA
    conv, group = pl.pallas_call(
        kernel,
        out_shape=(
            jax.ShapeDtypeStruct((27, 16, 128), F32),
            jax.ShapeDtypeStruct((72, 16), F32),
        ),
        in_specs=[hbm, hbm, vmem, smem, vmem],
        out_specs=(vmem, vmem),
        scratch_shapes=[
            pltpu.VMEM((4, 1024, 128), BF16),
            pltpu.VMEM((3, 1152, 256), BF16),
            pltpu.VMEM((4, 272, 1280), BF16),
            pltpu.VMEM((384, 256), BF16),
            pltpu.VMEM((2, 256, 256), BF16),
            pltpu.VMEM((9, 256, 256), BF16),
            pltpu.VMEM((3, 288, 256), BF16),
            pltpu.VMEM((3, 288, 256), BF16),
            pltpu.VMEM((2, 128, 256), BF16),
            pltpu.VMEM((2, 128, 128), BF16),
            pltpu.VMEM((128, 256), BF16),
            pltpu.VMEM((128, 128), BF16),
            pltpu.VMEM((16, 2, 128, 128), BF16),
            pltpu.VMEM((16, 2, 128, 128), BF16),
            pltpu.VMEM((8, 2, 16, 128), F32),
            pltpu.VMEM((8, 2, 16, 128), F32),
            pltpu.VMEM((2, 16, 128), F32),
            pltpu.VMEM((16, 2, 16, 128), F32),
            dma((2,)),
            dma((3,)),
            dma((3,)),
            dma((2,)),
            dma((2,)),
            dma((16,)),
            dma((16,)),
            dma((8,)),
            dma((8,)),
            dma((16,)),
            dma((16,)),
        ],
        compiler_params=pltpu.CompilerParams(
            collective_id=0, has_side_effects=True, vmem_limit_bytes=40 * 1024 * 1024
        ),
        cost_estimate=pl.CostEstimate(
            flops=2_500_000_000, bytes_accessed=3_000_000, transcendentals=0
        ),
    )(
        volume.reshape(1024, 128),
        conv_weight.reshape(3, 1152, 256),
        group_weight.reshape(9, 8, 256),
        slice_count,
        pooled_grad,
    )
    conv = conv.reshape(3, 3, 3, 16, 128).swapaxes(3, 4)
    return conv, group.reshape(3, 3, 8, 16)


def solution(mesh):
    in_specs = (P("vol", "sp", None, None, None), P(), P(), P("vol"), P("vol", None))
    out_specs = (P(None, None, None, None, "sp"), P(None, None, None, "sp"))
    return jax.shard_map(local, mesh=mesh, in_specs=in_specs, out_specs=out_specs, check_vma=False)
```

profile of v0, /device:TPU:8, one launch (start us, length us, event | category | flops | bytes accessed | tf_op | source)
XLA Modules:
  0.0 56.5 jit_solution(7116545617115149403)
XLA Ops:
  1.3 0.0 copy-start
  1.3 1.5 %copy-done = bf16[3,3,3,128,256]{4,3,2,1,0:T(8,128)(2,1)S(1)} copy-done((bf16[3,3,3,128,256]{4,3,2,1,0:T(8,128)(2,1)S(1)}, bf16[3,3,3,128,256]{4,3,2,1,0:T(8,128)(2,1)}, u32[]{:S(2)}) %copy-start) | copy-done | bytes 1769496
  2.8 0.0 copy-start.1
  2.8 0.9 %copy-done.1 = bf16[1,1,32,32,128]{4,3,2,1,0:T(8,128)(2,1)S(1)} copy-done((bf16[1,1,32,32,128]{4,3,2,1,0:T(8,128)(2,1)S(1)}, bf16[1,1,32,32,128]{4,3,2,1,0:T(8,128)(2,1)}, u32[]{:S(2)}) %copy-start.1) | copy-done | bytes 262168
  3.7 0.0 copy-start.2
  3.7 0.8 %copy-done.2 = bf16[3,3,8,256]{3,2,1,0:T(8,128)(2,1)S(1)} copy-done((bf16[3,3,8,256]{3,2,1,0:T(8,128)(2,1)S(1)}, bf16[3,3,8,256]{3,2,1,0:T(8,128)(2,1)}, u32[]{:S(2)}) %copy-start.2) | copy-done | bytes 36888
  4.5 0.0 copy-start.3
  4.5 0.7 %copy-done.3 = f32[1,256]{1,0:T(1,128)S(1)} copy-done((f32[1,256]{1,0:T(1,128)S(1)}, f32[1,256]{1,0:T(1,128)}, u32[]{:S(2)}) %copy-start.3) | copy-done | bytes 1048
  5.2 50.0 %shard_map.68 = (f32[27,16,128]{2,1,0:T(8,128)S(1)}, f32[72,16]{1,0:T(8,128)S(1)}) custom-call(bf16[1024,128]{1,0:T(8,128)(2,1)S(1)} %bitcast.10, bf16[3,1152,256]{2,1,0:T(8,128)(2,1)S(1)} %bitcast.9, bf16[9,8,256]{2,1,0:T(8,128)(2,1)S(1)} %bitcast.11, s32[1]{0:T(128)S(6)} %copy.9.cnt, f32[1,256]{1,0:T(1,128)S(1)} %copy-done.3), custom_call_target="tpu_custom_call" | custom-call | flops 2500000000 | bytes 3000000 | tf_op jit(solution)/shard_map/pallas_call | solution.py:363
  55.2 0.7 %copy.10 = f32[3,3,3,128,16]{3,4,2,1,0:T(8,128)} copy(f32[3,3,3,128,16]{3,4,2,1,0:T(8,128)S(1)} %bitcast.7) | data formatting | bytes 442368
  55.9 0.6 %copy.11 = f32[3,3,8,16]{3,2,1,0:T(8,128)} copy(f32[3,3,8,16]{3,2,1,0:T(8,128)S(1)} %bitcast.8) | data formatting | bytes 9216
Async XLA Ops:
  1.3 1.5 %copy-start = (bf16[3,3,3,128,256]{4,3,2,1,0:T(8,128)(2,1)S(1)}, bf16[3,3,3,128,256]{4,3,2,1,0:T(8,128)(2,1)}, u32[]{:S(2)}) copy-start(bf16[3,3,3,128,256]{4,3,2,1,0:T(8,128)(2,1)} %param.6) | copy-start | bytes 5308420
  2.8 0.9 %copy-start.1 = (bf16[1,1,32,32,128]{4,3,2,1,0:T(8,128)(2,1)S(1)}, bf16[1,1,32,32,128]{4,3,2,1,0:T(8,128)(2,1)}, u32[]{:S(2)}) copy-start(bf16[1,1,32,32,128]{4,3,2,1,0:T(8,128)(2,1)} %param.5) | copy-start | bytes 786436
  3.7 0.8 %copy-start.2 = (bf16[3,3,8,256]{3,2,1,0:T(8,128)(2,1)S(1)}, bf16[3,3,8,256]{3,2,1,0:T(8,128)(2,1)}, u32[]{:S(2)}) copy-start(bf16[3,3,8,256]{3,2,1,0:T(8,128)(2,1)} %param.7) | copy-start | bytes 110596
  4.5 0.7 %copy-start.3 = (f32[1,256]{1,0:T(1,128)S(1)}, f32[1,256]{1,0:T(1,128)}, u32[]{:S(2)}) copy-start(f32[1,256]{1,0:T(1,128)} %pg.1) | copy-start | bytes 3076
where the time goes:
time: 57.4 us; the launch traced here: 56.5 us
  Pallas kernels  50 us (87%)
  local copies, waits for them, and re-layouts  5.17 us (9%)
  between operations  1.3 us (2%)
    pallas_call x1, Pallas kernels, local(): pl.pallas_call(kernel, out_shape=(jax.ShapeDtypeStruct((27, 16, 128), F32...  50 us
    unnamed x10, local copies, waits for them, and re-layouts  5.17 us

commit v1 on v0

v1 whole, which is shorter than its diff:
```python
import jax
import jax.numpy as jnp
from jax import lax
from jax.experimental import pallas as pl
from jax.experimental.pallas import tpu as pltpu
from jax.sharding import PartitionSpec as P

BF16 = jnp.bfloat16
F32 = jnp.float32
CHUNKS = 4
Z_FIRST = ((5, 9), (5, 9), (6, 9))
VOL_NEAR_LAST = sorted(
    ((i, j) for i in range(4) for j in range(4) if i + j > 0),
    key=lambda o: -(min(o[0], 4 - o[0]) + min(o[1], 4 - o[1])),
)
Z_NEAR_LAST = (4, 3, 5, 2, 6, 1, 7)
Z_BLOCKS = 11


def remote(src, dst, send, recv, device):
    return pltpu.make_async_remote_copy(
        src_ref=src,
        dst_ref=dst,
        send_sem=send,
        recv_sem=recv,
        device_id=device,
        device_id_type=pl.DeviceIdType.MESH,
    )


def dot(left, right):
    return jnp.dot(left, right, preferred_element_type=F32)


def dot_nt(left, right):
    return lax.dot_general(left, right, (((1,), (1,)), ((), ())), preferred_element_type=F32)


def one_where(condition):
    return jnp.where(condition, 1.0, 0.0).astype(BF16)


def iota(shape, dim):
    return lax.broadcasted_iota(jnp.int32, shape, dim)


def kernel(
    vol,
    w,
    gw_hbm,
    cnt,
    pg_hbm,
    conv_out,
    group_out,
    volb,
    wv,
    gw,
    pg,
    xs,
    pick,
    shift,
    wg,
    hk,
    dk,
    dts,
    ggs,
    dx,
    gx,
    za,
    zr,
    ga,
    gr,
    va,
    vr,
    s2,
    r2,
    b2,
    rb2,
    f3,
    outb,
    loc_sem,
    sib_send,
    sib_recv,
    far_send,
    far_recv,
    dx_send,
    dx_recv,
    za_send,
    za_recv,
    ga_send,
    ga_recv,
    va_send,
    va_recv,
    s2_send,
    s2_recv,
    b2_send,
    b2_recv,
    f3_send,
    f3_recv,
):
    v = lax.axis_index("vol")
    sp = lax.axis_index("sp")
    x, y = lax.div(v, 4), lax.rem(v, 4)
    z, core = lax.div(sp, 2), lax.rem(sp, 2)
    sib = (v, z * 2 + 1 - core)
    far = (v, lax.rem(sp + 15 + 2 * core, 16))
    vol_peers = [lax.rem(x + i, 4) * 4 + lax.rem(y + j, 4) for i, j in VOL_NEAR_LAST]
    z_peers = [lax.rem(z + i, 8) for i in Z_NEAR_LAST]

    def at_z(k):
        return (v, k * 2 + core)

    own_copy = pltpu.make_async_copy(vol, volb.at[1 + core], loc_sem.at[0])
    own_copy.start()
    gw_copy = pltpu.make_async_copy(gw_hbm, gw, loc_sem.at[2])
    gw_copy.start()
    pg_copy = pltpu.make_async_copy(pg_hbm, pg, loc_sem.at[3])
    pg_copy.start()
    w_copy = pltpu.make_async_copy(w, wv, loc_sem.at[1])
    w_copy.start()

    barrier = pltpu.get_barrier_semaphore()
    for device in [sib, far] + [(k, sp) for k in vol_peers] + [at_z(k) for k in z_peers]:
        pl.semaphore_signal(barrier, inc=1, device_id=device, device_id_type=pl.DeviceIdType.MESH)

    m = iota((384, 256), 0)
    tap, within = lax.div(m, 128), lax.rem(m, 128)
    row = 2 * lax.div(lax.rem(within, 64), 16) + lax.div(within, 64)
    col = 2 * lax.rem(within, 16) + tap - 1
    pick[...] = one_where((iota((384, 256), 1) == row * 32 + col) & (col >= 0))

    pl.semaphore_wait(barrier, 24)

    def rows_of(chunk):
        return pl.ds(256 * chunk, 256)

    to_far = [
        remote(
            vol.at[rows_of(q)],
            volb.at[3 - 3 * core, rows_of(q)],
            far_send.at[q],
            far_recv.at[q],
            far,
        )
        for q in range(CHUNKS)
    ]
    to_sib = remote(vol, volb.at[1 + core], sib_send.at[0], sib_recv.at[0], sib)
    for copy in to_far:
        copy.start()
    to_sib.start()

    m, n = iota((256, 256), 0), iota((256, 256), 1)
    in_row = lax.rem(m, 16)
    shift[0] = one_where((n == m - 1) & (in_row != 0))
    shift[1] = one_where((n == m + 1) & (in_row != 15))
    same_group = lax.div(m, 8) == lax.div(n, 8)
    for k in range(3):
        hk[k, 0:16, :] = jnp.zeros((16, 256), BF16)
        hk[k, 272:288, :] = jnp.zeros((16, 256), BF16)
        dk[k, 0:16, :] = jnp.zeros((16, 256), BF16)
        dk[k, 272:288, :] = jnp.zeros((16, 256), BF16)

    def windows(slot, block, inside):
        if block == 0:
            xs[slot, 0:16, 0:384] = jnp.zeros((16, 384), BF16)
        picked = dot(pick[...], volb[slot, 256 * block : 256 * block + 256, :])
        if inside is not None:
            picked = picked * inside
        picked = picked.astype(BF16)
        for e in range(3):
            even = picked[e * 128 : e * 128 + 64]
            odd = picked[e * 128 + 64 : e * 128 + 128]
            for b, rows, offset in ((0, odd, 16), (1, even, 0), (2, odd, 0)):
                lane = (b * 3 + e) * 128
                start = 64 * block + offset
                xs[slot, start : start + 64, lane : lane + 128] = rows

    at_low = jnp.where(z == 0, 0.0, 1.0)
    at_high = jnp.where(z == 7, 0.0, 1.0)
    far_inside = jnp.where(core == 0, at_low, at_high)
    beyond_inside = jnp.where(core == 0, at_high, at_low)

    own_copy.wait()
    for block in range(4):
        windows(1 + core, block, None)
    gw_copy.wait()
    for jk in range(9):
        tiled = jnp.broadcast_to(gw[jk].astype(F32)[None], (32, 8, 256)).reshape(256, 256)
        wg[jk] = jnp.where(same_group, tiled, 0.0).astype(BF16)
    remote(vol, volb.at[2 - core], sib_send.at[0], sib_recv.at[0], sib).wait_recv()
    for block in range(4):
        windows(2 - core, block, None)
    w_copy.wait()
    pre = dot(xs[core + 1, 0:256, :], wv[1]) + dot(xs[2 - core, 0:256, :], wv[2 - 2 * core])
    for block in range(4):
        remote(
            vol.at[rows_of(block)],
            volb.at[3 * core, rows_of(block)],
            far_send.at[block],
            far_recv.at[block],
            far,
        ).wait_recv()
        windows(3 * core, block, far_inside)
    relay = remote(volb.at[3 * core], volb.at[3 * core], sib_send.at[1], sib_recv.at[1], sib)
    relay.start()
    pre = pre + dot(xs[3 * core, 0:256, :], wv[2 * core])

    pg_copy.wait()
    count = cnt[0]
    live = jnp.where(sp < count, 1.0, 0.0)
    hidden = (jnp.maximum(pre, 0.0) * live).astype(BF16)
    hk[1, 16:272, :] = hidden
    hk[0, 16:272, :] = dot(shift[0], hidden).astype(BF16)
    hk[2, 16:272, :] = dot(shift[1], hidden).astype(BF16)
    summed = hidden.astype(F32)
    for j in range(3):
        for k in range(3):
            summed = summed + dot(hk[k, 16 * j : 16 * j + 256, :], wg[3 * j + k])
    scale = 1.0 / jnp.full((1, 256), count.astype(F32) * 256.0)
    cotangent = pg[...] * live * scale
    d_wide = jnp.where(summed > 0, cotangent, 0.0)
    d_summed = d_wide.astype(BF16)
    dk[1, 16:272, :] = d_summed
    dk[0, 16:272, :] = dot(shift[0], d_summed).astype(BF16)
    dk[2, 16:272, :] = dot(shift[1], d_summed).astype(BF16)
    d_hidden = d_summed.astype(F32)
    for j in range(3):
        for k in range(3):
            lines = dk[2 - k, 16 * (2 - j) : 16 * (2 - j) + 256, :]
            d_hidden = d_hidden + dot_nt(lines, wg[3 * j + k])
    d_pre = jnp.where(pre > 0, d_hidden, 0.0) * live
    turned = d_pre.T.astype(BF16)
    for t in range(8):
        for c in range(2):
            start = 16 * (2 * t + c)
            dts[c, 16 * t : 16 * t + 16, :] = turned[start : start + 16, :]
    swap_d = remote(dts.at[1 - core], dx, dx_send.at[0], dx_recv.at[0], sib)
    swap_d.start()

    remote(
        volb.at[3 - 3 * core], volb.at[3 - 3 * core], sib_send.at[1], sib_recv.at[1], sib
    ).wait_recv()
    for block in range(4):
        windows(3 - 3 * core, block, beyond_inside)
    swap_d.wait_recv()

    def partial(a, first, end):
        lanes = slice(128 * first, 128 * end)
        total = dot(dts[core], xs[core + a, 0:256, lanes])
        return (total + dot(dx[...], xs[1 - core + a, 0:256, lanes])).astype(BF16)

    place = 0
    for a in range(3):
        first, end = Z_FIRST[a]
        total = partial(a, first, end)
        for q in range(end - first):
            for t in range(8):
                za[t, place + q] = total[16 * t : 16 * t + 16, 128 * q : 128 * q + 128]
        place += end - first
    z_sends = [
        remote(za.at[k], zr.at[z], za_send.at[k], za_recv.at[z], at_z(k)) for k in z_peers
    ]
    for copy in z_sends:
        copy.start()

    place = 0
    for a in range(3):
        first = Z_FIRST[a][0]
        total = partial(a, 0, first)
        for q in range(first):
            va[place + q] = total[:, 128 * q : 128 * q + 128]
        place += first
    v_sends = [
        remote(va.at[k], vr.at[v], va_send.at[k], va_recv.at[v], (k, sp)) for k in vol_peers
    ]
    for copy in v_sends:
        copy.start()

    d_turned = d_wide.T.astype(BF16)
    fold = one_where(lax.rem(iota((256, 128), 0), 8) == lax.rem(iota((256, 128), 1), 8))
    lane_tap = lax.div(iota((256, 128), 1), 8)
    grouped = jnp.zeros((256, 128), F32)
    for j in range(3):
        for k in range(3):
            full = dot(d_turned, hk[k, 16 * j : 16 * j + 256, :])
            kept = jnp.where(same_group, full, 0.0).astype(BF16)
            grouped = jnp.where(lane_tap == 3 * j + k, dot(kept, fold), grouped)
    grouped = grouped.astype(BF16)
    for t in range(8):
        for c in range(2):
            start = 16 * (2 * t + c)
            ggs[c, t] = grouped[start : start + 16, :]
    swap_g = remote(ggs.at[1 - core], gx, dx_send.at[1], dx_recv.at[1], sib)
    swap_g.start()
    swap_g.wait_recv()
    ga[...] = (ggs[core].astype(F32) + gx[...].astype(F32)).astype(BF16)
    g_sends = [
        remote(ga.at[k], gr.at[z], ga_send.at[k], ga_recv.at[z], at_z(k)) for k in z_peers
    ]
    for copy in g_sends:
        copy.start()

    total = va[v].astype(F32)
    for k in reversed(vol_peers):
        remote(va.at[0], vr.at[k], va_send.at[0], va_recv.at[k], (k, sp)).wait_recv()
        total = total + vr[k].astype(F32)
    for t in range(8):
        s2[t] = total[16 * t : 16 * t + 16, :]
    s2_sends = [
        remote(s2.at[k], r2.at[z], s2_send.at[k], s2_recv.at[z], at_z(k)) for k in z_peers
    ]
    for copy in s2_sends:
        copy.start()

    total = za[z].astype(F32)
    for k in reversed(z_peers):
        remote(za.at[0], zr.at[k], za_send.at[0], za_recv.at[k], at_z(k)).wait_recv()
        total = total + zr[k].astype(F32)
    b2[0:Z_BLOCKS] = total
    total = ga[z].astype(F32)
    for k in reversed(z_peers):
        remote(ga.at[0], gr.at[k], ga_send.at[0], ga_recv.at[k], at_z(k)).wait_recv()
        total = total + gr[k].astype(F32)
    b2[Z_BLOCKS] = total
    for k in vol_peers:

        @pl.when(k <= Z_BLOCKS)
        def _(k=k):
            remote(b2.at[k], rb2.at[v], b2_send.at[k], b2_recv.at[v], (k, sp)).start()

    total = s2[z]
    for k in reversed(z_peers):
        remote(s2.at[0], r2.at[k], s2_send.at[0], s2_recv.at[k], at_z(k)).wait_recv()
        total = total + r2[k]
    f3[0] = total
    outb[v, 0] = total

    @pl.when(v <= Z_BLOCKS)
    def _():
        total = b2[v]
        for k in reversed(vol_peers):
            remote(b2.at[0], rb2.at[k], b2_send.at[0], b2_recv.at[k], (k, sp)).wait_recv()
            total = total + rb2[k]
        f3[1] = total
        outb[v, 1] = total
        for k in vol_peers:
            remote(f3, outb.at[v], f3_send.at[k], f3_recv.at[v], (k, sp)).start()

    @pl.when(v > Z_BLOCKS)
    def _():
        for k in vol_peers:
            remote(f3.at[0], outb.at[v, 0], f3_send.at[k], f3_recv.at[v], (k, sp)).start()

    for k in reversed(vol_peers):

        @pl.when(k <= Z_BLOCKS)
        def _(k=k):
            remote(f3, outb.at[k], f3_send.at[0], f3_recv.at[k], (k, sp)).wait_recv()

        @pl.when(k > Z_BLOCKS)
        def _(k=k):
            remote(f3.at[0], outb.at[k, 0], f3_send.at[0], f3_recv.at[k], (k, sp)).wait_recv()

    by_vol, by_z = 0, 0
    for a in range(3):
        first, end = Z_FIRST[a]
        for t in range(first):
            conv_out[9 * a + t] = outb[by_vol, 0]
            by_vol += 1
        for t in range(first, end):
            conv_out[9 * a + t] = outb[by_z, 1]
            by_z += 1
    last = jnp.concatenate([outb[Z_BLOCKS, 1], jnp.zeros((112, 128), F32)], axis=0)
    group_out[...] = last.T[0:72, 0:16]

    for copy in to_far + [to_sib, relay, swap_d, swap_g] + z_sends + v_sends + g_sends + s2_sends:
        copy.wait_send()
    for k in vol_peers:

        @pl.when(k <= Z_BLOCKS)
        def _(k=k):
            remote(b2.at[k], rb2.at[v], b2_send.at[k], b2_recv.at[v], (k, sp)).wait_send()

        @pl.when(v <= Z_BLOCKS)
        def _(k=k):
            remote(f3, outb.at[v], f3_send.at[k], f3_recv.at[v], (k, sp)).wait_send()

        @pl.when(v > Z_BLOCKS)
        def _(k=k):
            remote(f3.at[0], outb.at[v, 0], f3_send.at[k], f3_recv.at[v], (k, sp)).wait_send()


def local(volume, conv_weight, group_weight, slice_count, pooled_grad):
    vmem = pl.BlockSpec(memory_space=pltpu.VMEM)
    smem = pl.BlockSpec(memory_space=pltpu.SMEM)
    hbm = pl.BlockSpec(memory_space=pltpu.HBM)
    dma = pltpu.SemaphoreType.DMA
    conv, group = pl.pallas_call(
        kernel,
        out_shape=(
            jax.ShapeDtypeStruct((27, 16, 128), F32),
            jax.ShapeDtypeStruct((72, 16), F32),
        ),
        in_specs=[hbm, hbm, hbm, smem, hbm],
        out_specs=(vmem, vmem),
        scratch_shapes=[
            pltpu.VMEM((4, 1024, 128), BF16),
            pltpu.VMEM((3, 1152, 256), BF16),
            pltpu.VMEM((9, 8, 256), BF16),
            pltpu.VMEM((1, 256), F32),
            pltpu.VMEM((4, 272, 1152), BF16),
            pltpu.VMEM((384, 256), BF16),
            pltpu.VMEM((2, 256, 256), BF16),
            pltpu.VMEM((9, 256, 256), BF16),
            pltpu.VMEM((3, 288, 256), BF16),
            pltpu.VMEM((3, 288, 256), BF16),
            pltpu.VMEM((2, 128, 256), BF16),
            pltpu.VMEM((2, 8, 16, 128), BF16),
            pltpu.VMEM((128, 256), BF16),
            pltpu.VMEM((8, 16, 128), BF16),
            pltpu.VMEM((8, Z_BLOCKS, 16, 128), BF16),
            pltpu.VMEM((8, Z_BLOCKS, 16, 128), BF16),
            pltpu.VMEM((8, 16, 128), BF16),
            pltpu.VMEM((8, 16, 128), BF16),
            pltpu.VMEM((16, 128, 128), BF16),
            pltpu.VMEM((16, 128, 128), BF16),
            pltpu.VMEM((8, 16, 128), F32),
            pltpu.VMEM((8, 16, 128), F32),
            pltpu.VMEM((Z_BLOCKS + 1, 16, 128), F32),
            pltpu.VMEM((16, 16, 128), F32),
            pltpu.VMEM((2, 16, 128), F32),
            pltpu.VMEM((16, 2, 16, 128), F32),
            dma((4,)),
            dma((2,)),
            dma((2,)),
            dma((CHUNKS,)),
            dma((CHUNKS,)),
            dma((2,)),
            dma((2,)),
            dma((8,)),
            dma((8,)),
            dma((8,)),
            dma((8,)),
            dma((16,)),
            dma((16,)),
            dma((8,)),
            dma((8,)),
            dma((16,)),
            dma((16,)),
            dma((16,)),
            dma((16,)),
        ],
        compiler_params=pltpu.CompilerParams(
            collective_id=0, has_side_effects=True, vmem_limit_bytes=56_000_000
        ),
        cost_estimate=pl.CostEstimate(
            flops=2_500_000_000, bytes_accessed=3_000_000, transcendentals=0
        ),
    )(
        volume.reshape(1024, 128),
        conv_weight.reshape(3, 1152, 256),
        group_weight.reshape(9, 8, 256),
        slice_count,
        pooled_grad,
    )
    conv = conv.reshape(3, 3, 3, 16, 128).swapaxes(3, 4)
    return conv, group.reshape(3, 3, 8, 16)


def solution(mesh):
    in_specs = (P("vol", "sp", None, None, None), P(), P(), P("vol"), P("vol", None))
    out_specs = (P(None, None, None, None, "sp"), P(None, None, None, "sp"))
    return jax.shard_map(local, mesh=mesh, in_specs=in_specs, out_specs=out_specs, check_vma=False)
```

time: 57.4 us -> 45.9 us (0.80)
  Pallas kernels: 50 us -> 41.2 us
  local copies, waits for them, and re-layouts: 5.17 us -> 2.74 us
    pallas_call x1, Pallas kernels: 50 us -> 41.2 us  [local(): pl.pallas_call(kernel, out_shape=(jax.ShapeDtypeStruct((27, 16, 128), F32...]
    unnamed x10 -> x6, local copies, waits for them, and re-layouts: 5.17 us -> 2.74 us
where the time goes in v1:
time: 45.9 us; the launch traced here: 45.3 us
  Pallas kernels  41.2 us (90%)
  local copies, waits for them, and re-layouts  2.74 us (6%)
  between operations  1.29 us (3%)
    pallas_call x1, Pallas kernels, local(): pl.pallas_call(kernel, out_shape=(jax.ShapeDtypeStruct((27, 16, 128), F32...  41.2 us
    unnamed x6, local copies, waits for them, and re-layouts  2.74 us

profile of v1, /device:TPU:8, one launch (start us, length us, event | category | flops | bytes accessed | tf_op | source)
XLA Modules:
  0.0 45.3 jit_solution(17978777418552707284)
XLA Ops:
  1.3 0.0 copy-start
  1.3 0.8 %copy-done = bf16[3,3,8,256]{3,2,1,0:T(8,128)(2,1)S(1)} copy-done((bf16[3,3,8,256]{3,2,1,0:T(8,128)(2,1)S(1)}, bf16[3,3,8,256]{3,2,1,0:T(8,128)(2,1)}, u32[]{:S(2)}) %copy-start) | copy-done | bytes 36888
  2.0 0.0 copy-start.1
  2.0 0.7 %copy-done.1 = f32[1,256]{1,0:T(1,128)S(1)} copy-done((f32[1,256]{1,0:T(1,128)S(1)}, f32[1,256]{1,0:T(1,128)}, u32[]{:S(2)}) %copy-start.1) | copy-done | bytes 1048
  2.7 41.2 %shard_map.68 = (f32[27,16,128]{2,1,0:T(8,128)S(1)}, f32[72,16]{1,0:T(8,128)S(1)}) custom-call(bf16[1024,128]{1,0:T(8,128)(2,1)} %bitcast.11, bf16[3,1152,256]{2,1,0:T(8,128)(2,1)} %bitcast.10, bf16[9,8,256]{2,1,0:T(8,128)(2,1)S(1)} %bitcast.9, s32[1]{0:T(128)S(6)} %copy.9.cnt, f32[1,256]{1,0:T(1,128)S(1)} %copy-done.1), custom_call_target="tpu_custom_call" | custom-call | flops 2500000000 | bytes 3000000 | tf_op jit(solution)/shard_map/pallas_call | solution.py:398
  44.0 0.7 %copy.10 = f32[3,3,3,128,16]{3,4,2,1,0:T(8,128)} copy(f32[3,3,3,128,16]{3,4,2,1,0:T(8,128)S(1)} %bitcast.7) | data formatting | bytes 442368
  44.6 0.6 %copy.11 = f32[3,3,8,16]{3,2,1,0:T(8,128)} copy(f32[3,3,8,16]{3,2,1,0:T(8,128)S(1)} %bitcast.8) | data formatting | bytes 9216
Async XLA Ops:
  1.3 0.8 %copy-start = (bf16[3,3,8,256]{3,2,1,0:T(8,128)(2,1)S(1)}, bf16[3,3,8,256]{3,2,1,0:T(8,128)(2,1)}, u32[]{:S(2)}) copy-start(bf16[3,3,8,256]{3,2,1,0:T(8,128)(2,1)} %param.7) | copy-start | bytes 110596
  2.0 0.7 %copy-start.1 = (f32[1,256]{1,0:T(1,128)S(1)}, f32[1,256]{1,0:T(1,128)}, u32[]{:S(2)}) copy-start(f32[1,256]{1,0:T(1,128)} %pg_hbm.1) | copy-start | bytes 3076

commit v2 on v1

--- a/solution.py
+++ b/solution.py
@@ -68,6 +68,7 @@
     gx,
     za,
     zr,
+    zm,
     ga,
     gr,
     va,
@@ -81,12 +82,16 @@
     loc_sem,
     sib_send,
     sib_recv,
+    relay_send,
+    relay_recv,
     far_send,
     far_recv,
     dx_send,
     dx_recv,
     za_send,
     za_recv,
+    zm_send,
+    zm_recv,
     ga_send,
     ga_recv,
     va_send,
@@ -110,6 +115,9 @@
     def at_z(k):
         return (v, k * 2 + core)
 
+    def along(places):
+        return lax.rem(z + 8 + (1 - 2 * core) * places, 8)
+
     own_copy = pltpu.make_async_copy(vol, volb.at[1 + core], loc_sem.at[0])
     own_copy.start()
     gw_copy = pltpu.make_async_copy(gw_hbm, gw, loc_sem.at[2])
@@ -192,6 +200,7 @@
         windows(2 - core, block, None)
     w_copy.wait()
     pre = dot(xs[core + 1, 0:256, :], wv[1]) + dot(xs[2 - core, 0:256, :], wv[2 - 2 * core])
+    relays = []
     for block in range(4):
         remote(
             vol.at[rows_of(block)],
@@ -200,9 +209,16 @@
             far_recv.at[block],
             far,
         ).wait_recv()
+        relay = remote(
+            volb.at[3 * core, rows_of(block)],
+            volb.at[3 * core, rows_of(block)],
+            relay_send.at[block],
+            relay_recv.at[block],
+            sib,
+        )
+        relay.start()
+        relays.append(relay)
         windows(3 * core, block, far_inside)
-    relay = remote(volb.at[3 * core], volb.at[3 * core], sib_send.at[1], sib_recv.at[1], sib)
-    relay.start()
     pre = pre + dot(xs[3 * core, 0:256, :], wv[2 * core])
 
     pg_copy.wait()
@@ -237,10 +253,14 @@
     swap_d = remote(dts.at[1 - core], dx, dx_send.at[0], dx_recv.at[0], sib)
     swap_d.start()
 
-    remote(
-        volb.at[3 - 3 * core], volb.at[3 - 3 * core], sib_send.at[1], sib_recv.at[1], sib
-    ).wait_recv()
     for block in range(4):
+        remote(
+            volb.at[3 - 3 * core, rows_of(block)],
+            volb.at[3 - 3 * core, rows_of(block)],
+            relay_send.at[block],
+            relay_recv.at[block],
+            sib,
+        ).wait_recv()
         windows(3 - 3 * core, block, beyond_inside)
     swap_d.wait_recv()
 
@@ -258,9 +278,15 @@
                 za[t, place + q] = total[16 * t : 16 * t + 16, 128 * q : 128 * q + 128]
         place += end - first
     z_sends = [
-        remote(za.at[k], zr.at[z], za_send.at[k], za_recv.at[z], at_z(k)) for k in z_peers
+        remote(
+            za.at[along(home)], zm.at[i], zm_send.at[i], zm_recv.at[i], at_z(along(stop))
+        )
+        for i, (home, stop) in enumerate(((4, 2), (3, 1), (-3, -1)))
+    ] + [
+        remote(za.at[along(o)], zr.at[i], za_send.at[i], za_recv.at[i], at_z(along(o)))
+        for i, o in enumerate((1, -1, 2, -2))
     ]
-    for copy in z_sends:
+    for copy in z_sends[:5]:
         copy.start()
 
     place = 0
@@ -300,12 +326,19 @@
     for copy in g_sends:
         copy.start()
 
+    for copy in z_sends[:3]:
+        copy.wait_recv()
+    za[along(2)] = (za[along(2)].astype(F32) + zm[0].astype(F32) + zm[1].astype(F32)).astype(BF16)
+    za[along(-2)] = (za[along(-2)].astype(F32) + zm[2].astype(F32)).astype(BF16)
+    for copy in z_sends[5:]:
+        copy.start()
+
     total = va[v].astype(F32)
     for k in reversed(vol_peers):
         remote(va.at[0], vr.at[k], va_send.at[0], va_recv.at[k], (k, sp)).wait_recv()
         total = total + vr[k].astype(F32)
     for t in range(8):
-        s2[t] = total[16 * t : 16 * t + 16, :]
+        s2[t] = total[16 * t : 16 * t + 16, :].astype(BF16)
     s2_sends = [
         remote(s2.at[k], r2.at[z], s2_send.at[k], s2_recv.at[z], at_z(k)) for k in z_peers
     ]
@@ -313,36 +346,36 @@
         copy.start()
 
     total = za[z].astype(F32)
-    for k in reversed(z_peers):
-        remote(za.at[0], zr.at[k], za_send.at[0], za_recv.at[k], at_z(k)).wait_recv()
-        total = total + zr[k].astype(F32)
-    b2[0:Z_BLOCKS] = total
+    for i in range(4):
+        z_sends[3 + i].wait_recv()
+        total = total + zr[i].astype(F32)
+    b2[0:Z_BLOCKS] = total.astype(BF16)
     total = ga[z].astype(F32)
     for k in reversed(z_peers):
         remote(ga.at[0], gr.at[k], ga_send.at[0], ga_recv.at[k], at_z(k)).wait_recv()
         total = total + gr[k].astype(F32)
-    b2[Z_BLOCKS] = total
+    b2[Z_BLOCKS] = total.astype(BF16)
     for k in vol_peers:
 
         @pl.when(k <= Z_BLOCKS)
         def _(k=k):
             remote(b2.at[k], rb2.at[v], b2_send.at[k], b2_recv.at[v], (k, sp)).start()
 
-    total = s2[z]
+    total = s2[z].astype(F32)
     for k in reversed(z_peers):
         remote(s2.at[0], r2.at[k], s2_send.at[0], s2_recv.at[k], at_z(k)).wait_recv()
-        total = total + r2[k]
-    f3[0] = total
-    outb[v, 0] = total
+        total = total + r2[k].astype(F32)
+    f3[0] = total.astype(BF16)
+    outb[v, 0] = total.astype(BF16)
 
     @pl.when(v <= Z_BLOCKS)
     def _():
-        total = b2[v]
+        total = b2[v].astype(F32)
         for k in reversed(vol_peers):
             remote(b2.at[0], rb2.at[k], b2_send.at[0], b2_recv.at[k], (k, sp)).wait_recv()
-            total = total + rb2[k]
-        f3[1] = total
-        outb[v, 1] = total
+            total = total + rb2[k].astype(F32)
+        f3[1] = total.astype(BF16)
+        outb[v, 1] = total.astype(BF16)
         for k in vol_peers:
             remote(f3, outb.at[v], f3_send.at[k], f3_recv.at[v], (k, sp)).start()
 
@@ -365,15 +398,15 @@
     for a in range(3):
         first, end = Z_FIRST[a]
         for t in range(first):
-            conv_out[9 * a + t] = outb[by_vol, 0]
+            conv_out[9 * a + t] = outb[by_vol, 0].astype(F32)
             by_vol += 1
         for t in range(first, end):
-            conv_out[9 * a + t] = outb[by_z, 1]
+            conv_out[9 * a + t] = outb[by_z, 1].astype(F32)
             by_z += 1
-    last = jnp.concatenate([outb[Z_BLOCKS, 1], jnp.zeros((112, 128), F32)], axis=0)
+    last = jnp.concatenate([outb[Z_BLOCKS, 1].astype(F32), jnp.zeros((112, 128), F32)], axis=0)
     group_out[...] = last.T[0:72, 0:16]
 
-    for copy in to_far + [to_sib, relay, swap_d, swap_g] + z_sends + v_sends + g_sends + s2_sends:
+    for copy in to_far + relays + [to_sib, swap_d, swap_g] + z_sends + v_sends + g_sends + s2_sends:
         copy.wait_send()
     for k in vol_peers:
 
@@ -419,26 +452,31 @@
             pltpu.VMEM((128, 256), BF16),
             pltpu.VMEM((8, 16, 128), BF16),
             pltpu.VMEM((8, Z_BLOCKS, 16, 128), BF16),
-            pltpu.VMEM((8, Z_BLOCKS, 16, 128), BF16),
+            pltpu.VMEM((4, Z_BLOCKS, 16, 128), BF16),
+            pltpu.VMEM((3, Z_BLOCKS, 16, 128), BF16),
             pltpu.VMEM((8, 16, 128), BF16),
             pltpu.VMEM((8, 16, 128), BF16),
             pltpu.VMEM((16, 128, 128), BF16),
             pltpu.VMEM((16, 128, 128), BF16),
-            pltpu.VMEM((8, 16, 128), F32),
-            pltpu.VMEM((8, 16, 128), F32),
-            pltpu.VMEM((Z_BLOCKS + 1, 16, 128), F32),
-            pltpu.VMEM((16, 16, 128), F32),
-            pltpu.VMEM((2, 16, 128), F32),
-            pltpu.VMEM((16, 2, 16, 128), F32),
+            pltpu.VMEM((8, 16, 128), BF16),
+            pltpu.VMEM((8, 16, 128), BF16),
+            pltpu.VMEM((Z_BLOCKS + 1, 16, 128), BF16),
+            pltpu.VMEM((16, 16, 128), BF16),
+            pltpu.VMEM((2, 16, 128), BF16),
+            pltpu.VMEM((16, 2, 16, 128), BF16),
             dma((4,)),
-            dma((2,)),
-            dma((2,)),
+            dma((1,)),
+            dma((1,)),
+            dma((CHUNKS,)),
+            dma((CHUNKS,)),
             dma((CHUNKS,)),
             dma((CHUNKS,)),
             dma((2,)),
             dma((2,)),
-            dma((8,)),
-            dma((8,)),
+            dma((4,)),
+            dma((4,)),
+            dma((3,)),
+            dma((3,)),
             dma((8,)),
             dma((8,)),
             dma((16,)),

time: 45.9 us -> 43 us (0.937)
  Pallas kernels: 41.2 us -> 38.8 us
    pallas_call x1, Pallas kernels: 41.2 us -> 38.8 us  [local(): pl.pallas_call(kernel, out_shape=(jax.ShapeDtypeStruct((27, 16, 128), F32...]
where the time goes in v2:
time: 43 us; the launch traced here: 42.8 us
  Pallas kernels  38.8 us (90%)
  local copies, waits for them, and re-layouts  2.74 us (6%)
  between operations  1.29 us (3%)
    pallas_call x1, Pallas kernels, local(): pl.pallas_call(kernel, out_shape=(jax.ShapeDtypeStruct((27, 16, 128), F32...  38.8 us
    unnamed x6, local copies, waits for them, and re-layouts  2.74 us

profile of v2, /device:TPU:8, one launch (start us, length us, event | category | flops | bytes accessed | tf_op | source)
XLA Modules:
  0.0 42.8 jit_solution(6530731697330001390)
XLA Ops:
  1.3 0.0 copy-start
  1.3 0.8 %copy-done = bf16[3,3,8,256]{3,2,1,0:T(8,128)(2,1)S(1)} copy-done((bf16[3,3,8,256]{3,2,1,0:T(8,128)(2,1)S(1)}, bf16[3,3,8,256]{3,2,1,0:T(8,128)(2,1)}, u32[]{:S(2)}) %copy-start) | copy-done | bytes 36888
  2.0 0.0 copy-start.1
  2.0 0.7 %copy-done.1 = f32[1,256]{1,0:T(1,128)S(1)} copy-done((f32[1,256]{1,0:T(1,128)S(1)}, f32[1,256]{1,0:T(1,128)}, u32[]{:S(2)}) %copy-start.1) | copy-done | bytes 1048
  2.7 38.8 %shard_map.68 = (f32[27,16,128]{2,1,0:T(8,128)S(1)}, f32[72,16]{1,0:T(8,128)S(1)}) custom-call(bf16[1024,128]{1,0:T(8,128)(2,1)} %bitcast.11, bf16[3,1152,256]{2,1,0:T(8,128)(2,1)} %bitcast.10, bf16[9,8,256]{2,1,0:T(8,128)(2,1)S(1)} %bitcast.9, s32[1]{0:T(128)S(6)} %copy.9.cnt, f32[1,256]{1,0:T(1,128)S(1)} %copy-done.1), custom_call_target="tpu_custom_call" | custom-call | flops 2500000000 | bytes 3000000 | tf_op jit(solution)/shard_map/pallas_call | solution.py:431
  41.5 0.7 %copy.10 = f32[3,3,3,128,16]{3,4,2,1,0:T(8,128)} copy(f32[3,3,3,128,16]{3,4,2,1,0:T(8,128)S(1)} %bitcast.7) | data formatting | bytes 442368
  42.2 0.6 %copy.11 = f32[3,3,8,16]{3,2,1,0:T(8,128)} copy(f32[3,3,8,16]{3,2,1,0:T(8,128)S(1)} %bitcast.8) | data formatting | bytes 9216
Async XLA Ops:
  1.3 0.8 %copy-start = (bf16[3,3,8,256]{3,2,1,0:T(8,128)(2,1)S(1)}, bf16[3,3,8,256]{3,2,1,0:T(8,128)(2,1)}, u32[]{:S(2)}) copy-start(bf16[3,3,8,256]{3,2,1,0:T(8,128)(2,1)} %param.7) | copy-start | bytes 110596
  2.0 0.7 %copy-start.1 = (f32[1,256]{1,0:T(1,128)S(1)}, f32[1,256]{1,0:T(1,128)}, u32[]{:S(2)}) copy-start(f32[1,256]{1,0:T(1,128)} %pg_hbm.1) | copy-start | bytes 3076

commit v3 on v2

--- a/solution.py
+++ b/solution.py
@@ -79,6 +79,7 @@
     rb2,
     f3,
     outb,
+    round_sem,
     loc_sem,
     sib_send,
     sib_recv,
@@ -127,9 +128,26 @@
     w_copy = pltpu.make_async_copy(w, wv, loc_sem.at[1])
     w_copy.start()
 
+    nearest = [
+        (lax.rem(x + 1, 4) * 4 + y, sp),
+        (lax.rem(x + 3, 4) * 4 + y, sp),
+        (x * 4 + lax.rem(y + 1, 4), sp),
+        (x * 4 + lax.rem(y + 3, 4), sp),
+        at_z(lax.rem(z + 1, 8)),
+        at_z(lax.rem(z + 7, 8)),
+    ]
     barrier = pltpu.get_barrier_semaphore()
-    for device in [sib, far] + [(k, sp) for k in vol_peers] + [at_z(k) for k in z_peers]:
+    for device in [sib, far] + nearest:
         pl.semaphore_signal(barrier, inc=1, device_id=device, device_id_type=pl.DeviceIdType.MESH)
+
+    def tell(i):
+        for device in nearest:
+            pl.semaphore_signal(
+                round_sem.at[i], inc=1, device_id=device, device_id_type=pl.DeviceIdType.MESH
+            )
+
+    def hear(i):
+        pl.semaphore_wait(round_sem.at[i], len(nearest))
 
     m = iota((384, 256), 0)
     tap, within = lax.div(m, 128), lax.rem(m, 128)
@@ -137,7 +155,7 @@
     col = 2 * lax.rem(within, 16) + tap - 1
     pick[...] = one_where((iota((384, 256), 1) == row * 32 + col) & (col >= 0))
 
-    pl.semaphore_wait(barrier, 24)
+    pl.semaphore_wait(barrier, 2 + len(nearest))
 
     def rows_of(chunk):
         return pl.ds(256 * chunk, 256)
@@ -156,6 +174,7 @@
     for copy in to_far:
         copy.start()
     to_sib.start()
+    tell(0)
 
     m, n = iota((256, 256), 0), iota((256, 256), 1)
     in_row = lax.rem(m, 16)
@@ -198,6 +217,8 @@
     remote(vol, volb.at[2 - core], sib_send.at[0], sib_recv.at[0], sib).wait_recv()
     for block in range(4):
         windows(2 - core, block, None)
+    hear(0)
+    tell(1)
     w_copy.wait()
     pre = dot(xs[core + 1, 0:256, :], wv[1]) + dot(xs[2 - core, 0:256, :], wv[2 - 2 * core])
     relays = []
@@ -221,6 +242,8 @@
         windows(3 * core, block, far_inside)
     pre = pre + dot(xs[3 * core, 0:256, :], wv[2 * core])
 
+    hear(1)
+    tell(2)
     pg_copy.wait()
     count = cnt[0]
     live = jnp.where(sp < count, 1.0, 0.0)
@@ -277,6 +300,7 @@
             for t in range(8):
                 za[t, place + q] = total[16 * t : 16 * t + 16, 128 * q : 128 * q + 128]
         place += end - first
+    hear(2)
     z_sends = [
         remote(
             za.at[along(home)], zm.at[i], zm_send.at[i], zm_recv.at[i], at_z(along(stop))
@@ -421,6 +445,10 @@
         @pl.when(v > Z_BLOCKS)
         def _(k=k):
             remote(f3.at[0], outb.at[v, 0], f3_send.at[k], f3_recv.at[v], (k, sp)).wait_send()
+
+
+def in_hbm(array):
+    return pltpu.with_memory_space_constraint(array, pltpu.HBM)
 
 
 def local(volume, conv_weight, group_weight, slice_count, pooled_grad):
@@ -464,6 +492,7 @@
             pltpu.VMEM((16, 16, 128), BF16),
             pltpu.VMEM((2, 16, 128), BF16),
             pltpu.VMEM((16, 2, 16, 128), BF16),
+            pltpu.SemaphoreType.REGULAR((3,)),
             dma((4,)),
             dma((1,)),
             dma((1,)),
@@ -489,17 +518,17 @@
             dma((16,)),
         ],
         compiler_params=pltpu.CompilerParams(
-            collective_id=0, has_side_effects=True, vmem_limit_bytes=56_000_000
+            collective_id=0, has_side_effects=True, vmem_limit_bytes=48_000_000
         ),
         cost_estimate=pl.CostEstimate(
             flops=2_500_000_000, bytes_accessed=3_000_000, transcendentals=0
         ),
     )(
-        volume.reshape(1024, 128),
-        conv_weight.reshape(3, 1152, 256),
-        group_weight.reshape(9, 8, 256),
+        in_hbm(volume.reshape(1024, 128)),
+        in_hbm(conv_weight.reshape(3, 1152, 256)),
+        in_hbm(group_weight.reshape(9, 8, 256)),
         slice_count,
-        pooled_grad,
+        in_hbm(pooled_grad),
     )
     conv = conv.reshape(3, 3, 3, 16, 128).swapaxes(3, 4)
     return conv, group.reshape(3, 3, 8, 16)

time: 43 us -> 40.5 us (0.942)
  local copies, waits for them, and re-layouts: 2.74 us -> 1.3 us
  Pallas kernels: 38.8 us -> 37.8 us
    unnamed x6 -> x2, local copies, waits for them, and re-layouts: 2.74 us -> 1.3 us
    pallas_call x1, Pallas kernels: 38.8 us -> 37.8 us  [local(): pl.pallas_call(kernel, out_shape=(jax.ShapeDtypeStruct((27, 16, 128), F32...]
where the time goes in v3:
time: 40.5 us; the launch traced here: 40.4 us
  Pallas kernels  37.8 us (93%)
  local copies, waits for them, and re-layouts  1.3 us (3%)
  between operations  1.29 us (3%)
    pallas_call x1, Pallas kernels, local(): pl.pallas_call(kernel, out_shape=(jax.ShapeDtypeStruct((27, 16, 128), F32...  37.8 us
    unnamed x2, local copies, waits for them, and re-layouts  1.3 us

profile of v3, /device:TPU:8, one launch (start us, length us, event | category | flops | bytes accessed | tf_op | source)
XLA Modules:
  0.0 40.4 jit_solution(12661072990195310442)
XLA Ops:
  1.3 37.8 %shard_map.68 = (f32[27,16,128]{2,1,0:T(8,128)S(1)}, f32[72,16]{1,0:T(8,128)S(1)}) custom-call(bf16[1024,128]{1,0:T(8,128)(2,1)} %bitcast.10, bf16[3,1152,256]{2,1,0:T(8,128)(2,1)} %bitcast.9, bf16[9,8,256]{2,1,0:T(8,128)(2,1)} %bitcast.11, s32[1]{0:T(128)S(6)} %copy.9.cnt, f32[1,256]{1,0:T(1,128)} %pg_hbm.1), custom_call_target="tpu_custom_call" | custom-call | flops 2500000000 | bytes 3000000 | tf_op jit(solution)/shard_map/pallas_call | solution.py:459
  39.1 0.7 %copy.10 = f32[3,3,3,128,16]{3,4,2,1,0:T(8,128)} copy(f32[3,3,3,128,16]{3,4,2,1,0:T(8,128)S(1)} %bitcast.7) | data formatting | bytes 442368
  39.8 0.6 %copy.11 = f32[3,3,8,16]{3,2,1,0:T(8,128)} copy(f32[3,3,8,16]{3,2,1,0:T(8,128)S(1)} %bitcast.8) | data formatting | bytes 9216

commit v4 on v3

--- a/solution.py
+++ b/solution.py
@@ -310,7 +310,7 @@
         remote(za.at[along(o)], zr.at[i], za_send.at[i], za_recv.at[i], at_z(along(o)))
         for i, o in enumerate((1, -1, 2, -2))
     ]
-    for copy in z_sends[:5]:
+    for copy in z_sends[:3]:
         copy.start()
 
     place = 0
@@ -318,10 +318,13 @@
         first = Z_FIRST[a][0]
         total = partial(a, 0, first)
         for q in range(first):
-            va[place + q] = total[:, 128 * q : 128 * q + 128]
+            for h in range(2):
+                va[h, place + q] = total[64 * h : 64 * h + 64, 128 * q : 128 * q + 128]
         place += first
     v_sends = [
-        remote(va.at[k], vr.at[v], va_send.at[k], va_recv.at[v], (k, sp)) for k in vol_peers
+        remote(va.at[h, k], vr.at[h, v], va_send.at[h, k], va_recv.at[h, v], (k, sp))
+        for h in range(2)
+        for k in vol_peers
     ]
     for copy in v_sends:
         copy.start()
@@ -350,6 +353,8 @@
     for copy in g_sends:
         copy.start()
 
+    for copy in z_sends[3:5]:
+        copy.start()
     for copy in z_sends[:3]:
         copy.wait_recv()
     za[along(2)] = (za[along(2)].astype(F32) + zm[0].astype(F32) + zm[1].astype(F32)).astype(BF16)
@@ -357,17 +362,25 @@
     for copy in z_sends[5:]:
         copy.start()
 
-    total = va[v].astype(F32)
-    for k in reversed(vol_peers):
-        remote(va.at[0], vr.at[k], va_send.at[0], va_recv.at[k], (k, sp)).wait_recv()
-        total = total + vr[k].astype(F32)
-    for t in range(8):
-        s2[t] = total[16 * t : 16 * t + 16, :].astype(BF16)
+    def over_z(h):
+        total = va[h, v].astype(F32)
+        for k in reversed(vol_peers):
+            remote(
+                va.at[0, 0], vr.at[h, k], va_send.at[h, 0], va_recv.at[h, k], (k, sp)
+            ).wait_recv()
+            total = total + vr[h, k].astype(F32)
+        for t in range(4):
+            s2[4 * h + t] = total[16 * t : 16 * t + 16, :].astype(BF16)
+        for copy, k in zip(s2_sends, z_peers):
+
+            @pl.when(lax.div(k, 4) == h)
+            def _(copy=copy):
+                copy.start()
+
     s2_sends = [
         remote(s2.at[k], r2.at[z], s2_send.at[k], s2_recv.at[z], at_z(k)) for k in z_peers
     ]
-    for copy in s2_sends:
-        copy.start()
+    over_z(0)
 
     total = za[z].astype(F32)
     for i in range(4):
@@ -385,6 +398,8 @@
         def _(k=k):
             remote(b2.at[k], rb2.at[v], b2_send.at[k], b2_recv.at[v], (k, sp)).start()
 
+    over_z(1)
+
     total = s2[z].astype(F32)
     for k in reversed(z_peers):
         remote(s2.at[0], r2.at[k], s2_send.at[0], s2_recv.at[k], at_z(k)).wait_recv()
@@ -407,6 +422,14 @@
     def _():
         for k in vol_peers:
             remote(f3.at[0], outb.at[v, 0], f3_send.at[k], f3_recv.at[v], (k, sp)).start()
+
+    for copy in to_far + relays + [to_sib, swap_d, swap_g] + z_sends + v_sends + g_sends + s2_sends:
+        copy.wait_send()
+    for k in vol_peers:
+
+        @pl.when(k <= Z_BLOCKS)
+        def _(k=k):
+            remote(b2.at[k], rb2.at[v], b2_send.at[k], b2_recv.at[v], (k, sp)).wait_send()
 
     for k in reversed(vol_peers):
 
@@ -430,20 +453,14 @@
     last = jnp.concatenate([outb[Z_BLOCKS, 1].astype(F32), jnp.zeros((112, 128), F32)], axis=0)
     group_out[...] = last.T[0:72, 0:16]
 
-    for copy in to_far + relays + [to_sib, swap_d, swap_g] + z_sends + v_sends + g_sends + s2_sends:
-        copy.wait_send()
-    for k in vol_peers:
-
-        @pl.when(k <= Z_BLOCKS)
-        def _(k=k):
-            remote(b2.at[k], rb2.at[v], b2_send.at[k], b2_recv.at[v], (k, sp)).wait_send()
-
-        @pl.when(v <= Z_BLOCKS)
-        def _(k=k):
+    @pl.when(v <= Z_BLOCKS)
+    def _():
+        for k in vol_peers:
             remote(f3, outb.at[v], f3_send.at[k], f3_recv.at[v], (k, sp)).wait_send()
 
-        @pl.when(v > Z_BLOCKS)
-        def _(k=k):
+    @pl.when(v > Z_BLOCKS)
+    def _():
+        for k in vol_peers:
             remote(f3.at[0], outb.at[v, 0], f3_send.at[k], f3_recv.at[v], (k, sp)).wait_send()
 
 
@@ -484,8 +501,8 @@
             pltpu.VMEM((3, Z_BLOCKS, 16, 128), BF16),
             pltpu.VMEM((8, 16, 128), BF16),
             pltpu.VMEM((8, 16, 128), BF16),
-            pltpu.VMEM((16, 128, 128), BF16),
-            pltpu.VMEM((16, 128, 128), BF16),
+            pltpu.VMEM((2, 16, 64, 128), BF16),
+            pltpu.VMEM((2, 16, 64, 128), BF16),
             pltpu.VMEM((8, 16, 128), BF16),
             pltpu.VMEM((8, 16, 128), BF16),
             pltpu.VMEM((Z_BLOCKS + 1, 16, 128), BF16),
@@ -508,8 +525,8 @@
             dma((3,)),
             dma((8,)),
             dma((8,)),
-            dma((16,)),
-            dma((16,)),
+            dma((2, 16)),
+            dma((2, 16)),
             dma((8,)),
             dma((8,)),
             dma((16,)),

time: 40.5 us -> 40.2 us (level)
  no operation moved by 1% of the time
where the time goes in v4:
time: 40.2 us; the launch traced here: 40.1 us
  Pallas kernels  37.5 us (93%)
  local copies, waits for them, and re-layouts  1.3 us (3%)
  between operations  1.29 us (3%)
    pallas_call x1, Pallas kernels, local(): pl.pallas_call(kernel, out_shape=(jax.ShapeDtypeStruct((27, 16, 128), F32...  37.5 us
    unnamed x2, local copies, waits for them, and re-layouts  1.3 us

profile of v4, /device:TPU:8, one launch (start us, length us, event | category | flops | bytes accessed | tf_op | source)
XLA Modules:
  0.0 40.1 jit_solution(17982023584097554619)
XLA Ops:
  1.3 37.5 %shard_map.68 = (f32[27,16,128]{2,1,0:T(8,128)S(1)}, f32[72,16]{1,0:T(8,128)S(1)}) custom-call(bf16[1024,128]{1,0:T(8,128)(2,1)} %bitcast.10, bf16[3,1152,256]{2,1,0:T(8,128)(2,1)} %bitcast.9, bf16[9,8,256]{2,1,0:T(8,128)(2,1)} %bitcast.11, s32[1]{0:T(128)S(6)} %copy.9.cnt, f32[1,256]{1,0:T(1,128)} %pg_hbm.1), custom_call_target="tpu_custom_call" | custom-call | flops 2500000000 | bytes 3000000 | tf_op jit(solution)/shard_map/pallas_call | solution.py:476
  38.8 0.7 %copy.10 = f32[3,3,3,128,16]{3,4,2,1,0:T(8,128)} copy(f32[3,3,3,128,16]{3,4,2,1,0:T(8,128)S(1)} %bitcast.7) | data formatting | bytes 442368
  39.4 0.6 %copy.11 = f32[3,3,8,16]{3,2,1,0:T(8,128)} copy(f32[3,3,8,16]{3,2,1,0:T(8,128)S(1)} %bitcast.8) | data formatting | bytes 9216

commit v5 on v4

--- a/solution.py
+++ b/solution.py
@@ -326,7 +326,7 @@
         for h in range(2)
         for k in vol_peers
     ]
-    for copy in v_sends:
+    for copy in v_sends[: len(vol_peers)]:
         copy.start()
 
     d_turned = d_wide.T.astype(BF16)
@@ -351,6 +351,8 @@
         remote(ga.at[k], gr.at[z], ga_send.at[k], ga_recv.at[z], at_z(k)) for k in z_peers
     ]
     for copy in g_sends:
+        copy.start()
+    for copy in v_sends[len(vol_peers) :]:
         copy.start()
 
     for copy in z_sends[3:5]:

time: 40.2 us -> 40.1 us (level)
  no operation moved by 1% of the time
where the time goes in v5:
time: 40.1 us; the launch traced here: 40 us
  Pallas kernels  37.4 us (93%)
  local copies, waits for them, and re-layouts  1.3 us (3%)
  between operations  1.29 us (3%)
    pallas_call x1, Pallas kernels, local(): pl.pallas_call(kernel, out_shape=(jax.ShapeDtypeStruct((27, 16, 128), F32...  37.4 us
    unnamed x2, local copies, waits for them, and re-layouts  1.3 us

profile of v5, /device:TPU:8, one launch (start us, length us, event | category | flops | bytes accessed | tf_op | source)
XLA Modules:
  0.0 40.0 jit_solution(4479397717484409787)
XLA Ops:
  1.3 37.4 %shard_map.68 = (f32[27,16,128]{2,1,0:T(8,128)S(1)}, f32[72,16]{1,0:T(8,128)S(1)}) custom-call(bf16[1024,128]{1,0:T(8,128)(2,1)} %bitcast.10, bf16[3,1152,256]{2,1,0:T(8,128)(2,1)} %bitcast.9, bf16[9,8,256]{2,1,0:T(8,128)(2,1)} %bitcast.11, s32[1]{0:T(128)S(6)} %copy.9.cnt, f32[1,256]{1,0:T(1,128)} %pg_hbm.1), custom_call_target="tpu_custom_call" | custom-call | flops 2500000000 | bytes 3000000 | tf_op jit(solution)/shard_map/pallas_call | solution.py:478
  38.7 0.7 %copy.10 = f32[3,3,3,128,16]{3,4,2,1,0:T(8,128)} copy(f32[3,3,3,128,16]{3,4,2,1,0:T(8,128)S(1)} %bitcast.7) | data formatting | bytes 442368
  39.4 0.6 %copy.11 = f32[3,3,8,16]{3,2,1,0:T(8,128)} copy(f32[3,3,8,16]{3,2,1,0:T(8,128)S(1)} %bitcast.8) | data formatting | bytes 9216

commit v6 on v4

--- a/solution.py
+++ b/solution.py
@@ -407,6 +407,17 @@
     f3[0] = total.astype(BF16)
     outb[v, 0] = total.astype(BF16)
 
+    by_vol = [
+        remote(f3.at[0], outb.at[v, 0], f3_send.at[0, k], f3_recv.at[0, v], (k, sp))
+        for k in vol_peers
+    ]
+    by_z = [
+        remote(f3.at[1], outb.at[v, 1], f3_send.at[1, k], f3_recv.at[1, v], (k, sp))
+        for k in vol_peers
+    ]
+    for copy in by_vol:
+        copy.start()
+
     @pl.when(v <= Z_BLOCKS)
     def _():
         total = b2[v].astype(F32)
@@ -415,13 +426,8 @@
             total = total + rb2[k].astype(F32)
         f3[1] = total.astype(BF16)
         outb[v, 1] = total.astype(BF16)
-        for k in vol_peers:
-            remote(f3, outb.at[v], f3_send.at[k], f3_recv.at[v], (k, sp)).start()
-
-    @pl.when(v > Z_BLOCKS)
-    def _():
-        for k in vol_peers:
-            remote(f3.at[0], outb.at[v, 0], f3_send.at[k], f3_recv.at[v], (k, sp)).start()
+        for copy in by_z:
+            copy.start()
 
     for copy in to_far + relays + [to_sib, swap_d, swap_g] + z_sends + v_sends + g_sends + s2_sends:
         copy.wait_send()
@@ -432,36 +438,37 @@
             remote(b2.at[k], rb2.at[v], b2_send.at[k], b2_recv.at[v], (k, sp)).wait_send()
 
     for k in reversed(vol_peers):
+        remote(
+            f3.at[0], outb.at[k, 0], f3_send.at[0, 0], f3_recv.at[0, k], (k, sp)
+        ).wait_recv()
+    place = 0
+    for a in range(3):
+        for t in range(Z_FIRST[a][0]):
+            conv_out[9 * a + t] = outb[place, 0].astype(F32)
+            place += 1
+    for copy in by_vol:
+        copy.wait_send()
+
+    for k in reversed(vol_peers):
 
         @pl.when(k <= Z_BLOCKS)
         def _(k=k):
-            remote(f3, outb.at[k], f3_send.at[0], f3_recv.at[k], (k, sp)).wait_recv()
-
-        @pl.when(k > Z_BLOCKS)
-        def _(k=k):
-            remote(f3.at[0], outb.at[k, 0], f3_send.at[0], f3_recv.at[k], (k, sp)).wait_recv()
-
-    by_vol, by_z = 0, 0
+            remote(
+                f3.at[1], outb.at[k, 1], f3_send.at[1, 0], f3_recv.at[1, k], (k, sp)
+            ).wait_recv()
+
+    place = 0
     for a in range(3):
-        first, end = Z_FIRST[a]
-        for t in range(first):
-            conv_out[9 * a + t] = outb[by_vol, 0].astype(F32)
-            by_vol += 1
-        for t in range(first, end):
-            conv_out[9 * a + t] = outb[by_z, 1].astype(F32)
-            by_z += 1
+        for t in range(*Z_FIRST[a]):
+            conv_out[9 * a + t] = outb[place, 1].astype(F32)
+            place += 1
     last = jnp.concatenate([outb[Z_BLOCKS, 1].astype(F32), jnp.zeros((112, 128), F32)], axis=0)
     group_out[...] = last.T[0:72, 0:16]
 
     @pl.when(v <= Z_BLOCKS)
     def _():
-        for k in vol_peers:
-            remote(f3, outb.at[v], f3_send.at[k], f3_recv.at[v], (k, sp)).wait_send()
-
-    @pl.when(v > Z_BLOCKS)
-    def _():
-        for k in vol_peers:
-            remote(f3.at[0], outb.at[v, 0], f3_send.at[k], f3_recv.at[v], (k, sp)).wait_send()
+        for copy in by_z:
+            copy.wait_send()
 
 
 def in_hbm(array):
@@ -531,8 +538,8 @@
             dma((8,)),
             dma((16,)),
             dma((16,)),
-            dma((16,)),
-            dma((16,)),
+            dma((2, 16)),
+            dma((2, 16)),
         ],
         compiler_params=pltpu.CompilerParams(
             collective_id=0, has_side_effects=True, vmem_limit_bytes=48_000_000

time: 40.2 us -> 40.4 us (level)
  no operation moved by 1% of the time
where the time goes in v6:
time: 40.4 us; the launch traced here: 40.3 us
  Pallas kernels  37.7 us (93%)
  local copies, waits for them, and re-layouts  1.3 us (3%)
  between operations  1.29 us (3%)
    pallas_call x1, Pallas kernels, local(): pl.pallas_call(kernel, out_shape=(jax.ShapeDtypeStruct((27, 16, 128), F32...  37.7 us
    unnamed x2, local copies, waits for them, and re-layouts  1.3 us

profile of v6, /device:TPU:8, one launch (start us, length us, event | category | flops | bytes accessed | tf_op | source)
XLA Modules:
  0.0 40.3 jit_solution(6590781245394343239)
XLA Ops:
  1.3 37.7 %shard_map.68 = (f32[27,16,128]{2,1,0:T(8,128)S(1)}, f32[72,16]{1,0:T(8,128)S(1)}) custom-call(bf16[1024,128]{1,0:T(8,128)(2,1)} %bitcast.10, bf16[3,1152,256]{2,1,0:T(8,128)(2,1)} %bitcast.9, bf16[9,8,256]{2,1,0:T(8,128)(2,1)} %bitcast.11, s32[1]{0:T(128)S(6)} %copy.9.cnt, f32[1,256]{1,0:T(1,128)} %pg_hbm.1), custom_call_target="tpu_custom_call" | custom-call | flops 2500000000 | bytes 3000000 | tf_op jit(solution)/shard_map/pallas_call | solution.py:483
  39.0 0.7 %copy.10 = f32[3,3,3,128,16]{3,4,2,1,0:T(8,128)} copy(f32[3,3,3,128,16]{3,4,2,1,0:T(8,128)S(1)} %bitcast.7) | data formatting | bytes 442368
  39.7 0.6 %copy.11 = f32[3,3,8,16]{3,2,1,0:T(8,128)} copy(f32[3,3,8,16]{3,2,1,0:T(8,128)S(1)} %bitcast.8) | data formatting | bytes 9216
